TPU v7x, 128 devices: a whole 4x4x4 slice. The times are simulated.
128 devices in a mesh: blk: 128 (over x, z, y, core).
Axes of the slice: x: 4, y: 4, z: 4, core: 2. Of those that a mesh axis runs over, the one named last changes fastest.
Arguments:
- embeddings: bfloat16 [49152, 768], P('blk'), may hold values from -6 to 6
- log_norms: bfloat16 [49152], P('blk'), may hold values from 6.5 to 9.5
- destinations: int32 [49152, 1], P('blk'), may hold values from 0 to 127; in each aligned block of 384 rows (0 to 383, 384 to 767, ...) at most 5 rows name the same one
- centroids: bfloat16 [262144, 768], P('blk'), may hold values from -6 to 6
Outputs:
- new_centroids: bfloat16 [262144, 768], P('blk')
Inputs may be any that keep to these rules, and one draw needn't show every extreme that they name: `destinations`: among the 384 rows of one reader, no device is named more than 5 times; some device is named exactly 5 times.
All inputs are finite; a program needn't handle non-finite values.
Results may differ from a plain program's by a relative error of at most 0.0042.
Values may be sent and summed in bfloat16 or wider, within the bound.
A program may use at most 64 MiB of HBM per device.

v0:
```python
import jax
import jax.numpy as jnp
from jax import lax
from jax.sharding import PartitionSpec as P

STOPS = 2


def from_behind(block, axis, distance):
    devices = range(lax.axis_size(axis))
    route = [((i - distance) % len(devices), i) for i in devices]
    return lax.ppermute(block, axis, route)


def contribute(panel, rows, lse, sums, counts):
    scale = rows.shape[1] ** (-0.5)
    scores = jnp.dot(rows, panel.T, preferred_element_type=jnp.float32) * scale
    resp = jnp.exp(scores - lse.astype(jnp.float32)[:, None])
    counts = counts + jnp.sum(resp, axis=0)
    resp_low = resp.astype(jnp.bfloat16)
    sums = sums + lax.dot_general(
        resp_low, rows, (((0,), (0,)), ((), ())), preferred_element_type=jnp.float32
    )
    return (sums, counts)


def body(embeddings, log_norms, destinations, centroids):
    devices = lax.axis_size("blk")
    pool = embeddings.shape[0]
    width = embeddings.shape[1]
    capacity = max(2, (3 * pool + 2 * devices - 1) // (2 * devices))
    dest = destinations[:, 0]
    onehot = (dest[:, None] == jnp.arange(devices, dtype=jnp.int32)[None, :]).astype(jnp.int32)
    rank = jnp.sum((jnp.cumsum(onehot, axis=0) - onehot) * onehot, axis=1)
    target = dest * capacity + rank
    source = (
        jnp.full((devices * capacity,), pool, jnp.int32)
        .at[target]
        .set(jnp.arange(pool, dtype=jnp.int32))
    )
    padded_rows = jnp.concatenate([embeddings, jnp.zeros((1, width), embeddings.dtype)], axis=0)
    padded_lse = jnp.concatenate([log_norms, jnp.full((1,), 10000.0, log_norms.dtype)], axis=0)
    send_rows = padded_rows[source]
    send_lse = padded_lse[source]
    rows, lse = (
        lax.all_to_all(send_rows, "blk", split_axis=0, concat_axis=0, tiled=True),
        lax.all_to_all(send_lse, "blk", split_axis=0, concat_axis=0, tiled=True),
    )
    panel_rows = centroids.shape[0]
    sums = jnp.zeros((panel_rows, width), jnp.float32)
    counts = jnp.zeros((panel_rows,), jnp.float32)
    sums, counts = contribute(centroids, rows, lse, sums, counts)
    panel = centroids
    for stop in range(STOPS):
        panel = from_behind(panel, "blk", 1)
        sums, counts = from_behind((sums, counts), "blk", 1)
        sums, counts = contribute(panel, rows, lse, sums, counts)
    sums, counts = from_behind((sums, counts), "blk", -2)
    fresh = (sums + centroids.astype(jnp.float32)) / (counts + 1.0)[:, None]
    return fresh.astype(jnp.bfloat16)


def solution(mesh):
    return jax.shard_map(
        body,
        mesh=mesh,
        in_specs=(P("blk", None), P("blk"), P("blk", None), P("blk", None)),
        out_specs=P("blk", None),
        check_vma=False,
    )
```

profile of v0, /device:TPU:0, one launch (start us, length us, event | category | flops | bytes accessed | tf_op | source)
XLA Modules:
  0.0 444.7 jit_solution(5564492838088975863)
XLA Ops:
  0.0 0.7 reduce
  0.7 0.1 copy.8
  0.8 0.2 fusion.17
  1.1 0.1 broadcast_add_fusion
  1.1 0.2 fusion.20
  1.4 0.7 fusion.24
  2.1 2.9 scatter_custom_fusion
  5.0 0.7 pad_maximum_fusion
  5.7 4.3 gather_fusion.1
  10.0 0.9 all_to_all.19
  10.9 11.1 %all-to-all-start.1 = ((bf16[128,5,1]{1,2,0:T(2,128)(2,1)}), bf16[128,5,1]{1,2,0:T(2,128)(2,1)S(1)}, u32[]{:S(2)}, u32[]{:S(2)}) async-start(bf16[128,5,1]{1,2,0:T(2,128)(2,1)} %all_to_all.19), calls=%async_computation.1 | async-start | bytes 131072 | tf_op jit(solution)/shard_map/all_to_all | solution.py:47
  22.1 1.1 concatenate.6
  23.2 3.0 gather_fusion
  26.1 1.3 all_to_all.14
  27.5 3.9 all-to-all-done.1
  31.4 5.9 %all-to-all-start = ((bf16[128,5,768]{2,1,0:T(8,128)(2,1)}), bf16[128,5,768]{2,1,0:T(8,128)(2,1)S(1)}, u32[]{:S(2)}, u32[]{:S(2)}) async-start(bf16[128,5,768]{2,1,0:T(8,128)(2,1)} %all_to_all.14), calls=%async_computation | async-start | bytes 3145728 | tf_op jit(solution)/shard_map/all_to_all | solution.py:46
  37.3 0.2 convert_reduce_fusion
  37.4 0.2 reshape.30
  37.7 24.4 %all-to-all-done = bf16[128,5,768]{2,1,0:T(8,128)(2,1)S(1)} async-done(((bf16[128,5,768]{2,1,0:T(8,128)(2,1)}), bf16[128,5,768]{2,1,0:T(8,128)(2,1)S(1)}, u32[]{:S(2)}, u32[]{:S(2)}) %all-to-all-start) | async-done | bytes 983072 | tf_op jit(solution)/shard_map/all_to_all | solution.py:46
  62.0 0.4 all_to_all.16
  62.5 0.0 copy-start
  62.5 4.5 %fusion.28 = f32[640,2048]{1,0:T(8,128)S(1)} fusion(bf16[640,768]{1,0:T(8,128)(2,1)S(1)} %all_to_all.16, bf16[2048,768]{1,0:T(8,128)(2,1)} %param.7), kind=kOutput, calls=%fused_computation.44 | convolution fusion | flops 2013265920 | bytes 9371648 | tf_op jit(solution)/shard_map/dot_general | solution.py:17
  67.0 0.0 copy-start.1
  67.0 3.1 fusion.9
  70.1 0.1 collective-permute-start
  70.2 0.6 copy-done.1
  70.8 0.0 collective-permute-start.1
  70.8 108.9 %collective-permute-done.1 = bf16[2048,768]{1,0:T(8,128)(2,1)S(1)} collective-permute-done((bf16[2048,768]{1,0:T(8,128)(2,1)S(1)}, bf16[2048,768]{1,0:T(8,128)(2,1)S(1)}, u32[]{:S(2)}, u32[]{:S(2)}) %collective-permute-start.1) | collective-permute-done | bytes 3145760 | tf_op jit(solution)/shard_map/ppermute | solution.py:12
  179.7 2.2 fusion.29
  181.9 0.0 copy-done.2
  181.9 0.0 collective-permute-done
  181.9 3.1 convolution_add_fusion
  185.1 0.1 collective-permute-start.2
  185.2 0.1 collective-permute-start.3
  185.2 109.4 %collective-permute-done.3 = bf16[2048,768]{1,0:T(8,128)(2,1)S(1)} collective-permute-done((bf16[2048,768]{1,0:T(8,128)(2,1)S(1)}, bf16[2048,768]{1,0:T(8,128)(2,1)S(1)}, u32[]{:S(2)}, u32[]{:S(2)}) %collective-permute-start.3) | collective-permute-done | bytes 3145760 | tf_op jit(solution)/shard_map/ppermute | solution.py:12
  294.7 6.5 %fusion.4 = (f32[2048]{0:T(1024)S(1)}, f32[2048]{0:T(1024)S(1)}, f32[2048]{0:T(1024)S(1)}, f32[640,2048]{1,0:T(8,128)S(1)}) fusion(f32[640]{0:T(1024)S(1)} %reshape.30, f32[640,2048]{1,0:T(8,128)} %copy-done.2, f32[640,2048]{1,0:T(8,128)S(1)} %fusion.29, bf16[640,768]{1,0:T(8,128)(2,1)S(1)} %all_to_all.16, bf16[2048,768]{1,0:T(8,128)(2,1)S(1)} %collective-permute-done.3), kind=kOutput, calls=%fused_computation.11 | convolution fusion | flops 2025056256 | bytes 19884544 | tf_op jit(solution)/shard_map/dot_general | solution.py:17
  301.2 4.3 fusion.6
  305.5 0.0 collective-permute-done.2
  305.5 0.8 add.43
  306.3 0.1 collective-permute-start.4
  306.4 0.1 collective-permute-start.5
  306.5 8.5 %collective-permute-done.5 = f32[2048]{0:T(1024)S(1)} collective-permute-done((f32[2048]{0:T(1024)S(1)}, f32[2048]{0:T(1024)S(1)}, u32[]{:S(2)}, u32[]{:S(2)}) %collective-permute-start.5) | collective-permute-done | bytes 8224 | tf_op jit(solution)/shard_map/ppermute | solution.py:12
  315.0 0.0 collective-permute-start.6
  315.0 8.5 %collective-permute-done.6 = f32[2048]{0:T(1024)S(1)} collective-permute-done((f32[2048]{0:T(1024)S(1)}, f32[2048]{0:T(1024)S(1)}, u32[]{:S(2)}, u32[]{:S(2)}) %collective-permute-start.6) | collective-permute-done | bytes 8224 | tf_op jit(solution)/shard_map/ppermute | solution.py:12
  323.5 0.0 collective-permute-start.7
  323.5 117.7 %collective-permute-done.7 = f32[2048]{0:T(1024)S(1)} collective-permute-done((f32[2048]{0:T(1024)S(1)}, f32[2048]{0:T(1024)S(1)}, u32[]{:S(2)}, u32[]{:S(2)}) %collective-permute-start.7) | collective-permute-done | bytes 8224 | tf_op jit(solution)/shard_map/ppermute | solution.py:12
  441.2 0.0 collective-permute-done.4
  441.2 3.5 divide_convert_fusion
  (11 shorter events, 0.1 us)
Async XLA Ops:
  10.9 20.4 %all-to-all-start.1 = ((bf16[128,5,1]{1,2,0:T(2,128)(2,1)}), bf16[128,5,1]{1,2,0:T(2,128)(2,1)S(1)}, u32[]{:S(2)}, u32[]{:S(2)}) async-start(bf16[128,5,1]{1,2,0:T(2,128)(2,1)} %all_to_all.19), calls=%async_computation.1 | async-start | bytes 131072 | tf_op jit(solution)/shard_map/all_to_all | solution.py:47
  31.4 30.7 %all-to-all-start = ((bf16[128,5,768]{2,1,0:T(8,128)(2,1)}), bf16[128,5,768]{2,1,0:T(8,128)(2,1)S(1)}, u32[]{:S(2)}, u32[]{:S(2)}) async-start(bf16[128,5,768]{2,1,0:T(8,128)(2,1)} %all_to_all.14), calls=%async_computation | async-start | bytes 3145728 | tf_op jit(solution)/shard_map/all_to_all | solution.py:46
  62.5 232.2 %copy-start = (bf16[640,768]{1,0:T(8,128)(2,1)}, bf16[640,768]{1,0:T(8,128)(2,1)S(1)}, u32[]{:S(2)}) copy-start(bf16[640,768]{1,0:T(8,128)(2,1)S(1)} %all_to_all.16) | copy-start | bytes 2949124
  67.0 115.0 %copy-start.2 = (f32[640,2048]{1,0:T(8,128)}, f32[640,2048]{1,0:T(8,128)S(1)}, u32[]{:S(2)}) copy-start(f32[640,2048]{1,0:T(8,128)S(1)} %fusion.28) | copy-start | bytes 15728644
  67.0 3.8 copy-start.1
  70.1 111.8 %collective-permute-start = (f32[2048,768]{1,0:T(8,128)S(1)}, f32[2048,768]{1,0:T(8,128)S(1)}, u32[]{:S(2)}, u32[]{:S(2)}) collective-permute-start(f32[2048,768]{1,0:T(8,128)S(1)} %fusion.9), channel_id=1, source_target_pairs={{127,0},{0,1},{1,2},{2,3},{3,4},{4,5},{5,6},{6,7},{7,8},{8,9},{9,1... | collective-permute-start | bytes 18874376 | tf_op jit(solution)/shard_map/ppermute | solution.py:12
  70.8 108.9 %collective-permute-start.1 = (bf16[2048,768]{1,0:T(8,128)(2,1)S(1)}, bf16[2048,768]{1,0:T(8,128)(2,1)S(1)}, u32[]{:S(2)}, u32[]{:S(2)}) collective-permute-start(bf16[2048,768]{1,0:T(8,128)(2,1)S(1)} %copy-done.1), channel_id=1, source_target_pairs={{127,0},{0,1},{1,2},{2,3},{3,4},{4,5},{5,6},{6,7},{7,8},{8,9},{9,1... | collective-permute-start | bytes 9437192 | tf_op jit(solution)/shard_map/ppermute | solution.py:12
  185.1 120.5 %collective-permute-start.2 = (f32[2048,768]{1,0:T(8,128)S(1)}, f32[2048,768]{1,0:T(8,128)S(1)}, u32[]{:S(2)}, u32[]{:S(2)}) collective-permute-start(f32[2048,768]{1,0:T(8,128)S(1)} %convolution_add_fusion), channel_id=1, source_target_pairs={{127,0},{0,1},{1,2},{2,3},{3,4},{4,5},{5,6},{6,7},{7,8},{8,9},{9,1... | collective-permute-start | bytes 18874376 | tf_op jit(solution)/shard_map/ppermute | solution.py:12
  185.2 109.5 %collective-permute-start.3 = (bf16[2048,768]{1,0:T(8,128)(2,1)S(1)}, bf16[2048,768]{1,0:T(8,128)(2,1)S(1)}, u32[]{:S(2)}, u32[]{:S(2)}) collective-permute-start(bf16[2048,768]{1,0:T(8,128)(2,1)S(1)} %collective-permute-done.1), channel_id=1, source_target_pairs={{127,0},{0,1},{1,2},{2,3},{3,4},{4,5},{5,6},{6,7},{7,8},{8,9},{9,1... | collective-permute-start | bytes 9437192 | tf_op jit(solution)/shard_map/ppermute | solution.py:12
  306.3 134.8 %collective-permute-start.4 = (f32[2048,768]{1,0:T(8,128)S(1)}, f32[2048,768]{1,0:T(8,128)S(1)}, u32[]{:S(2)}, u32[]{:S(2)}) collective-permute-start(f32[2048,768]{1,0:T(8,128)S(1)} %add.43), channel_id=1, source_target_pairs={{2,0},{3,1},{4,2},{5,3},{6,4},{7,5},{8,6},{9,7},{10,8},{11,9},{12,... | collective-permute-start | bytes 18874376 | tf_op jit(solution)/shard_map/ppermute | solution.py:12
  306.4 8.6 %collective-permute-start.5 = (f32[2048]{0:T(1024)S(1)}, f32[2048]{0:T(1024)S(1)}, u32[]{:S(2)}, u32[]{:S(2)}) collective-permute-start(f32[2048]{0:T(1024)S(1)} %get-tuple-element.6), channel_id=1, source_target_pairs={{127,0},{0,1},{1,2},{2,3},{3,4},{4,5},{5,6},{6,7},{7,8},{8,9},{9,1... | collective-permute-start | bytes 24584 | tf_op jit(solution)/shard_map/ppermute | solution.py:12
  315.0 8.5 %collective-permute-start.6 = (f32[2048]{0:T(1024)S(1)}, f32[2048]{0:T(1024)S(1)}, u32[]{:S(2)}, u32[]{:S(2)}) collective-permute-start(f32[2048]{0:T(1024)S(1)} %add.45), channel_id=1, source_target_pairs={{127,0},{0,1},{1,2},{2,3},{3,4},{4,5},{5,6},{6,7},{7,8},{8,9},{9,1... | collective-permute-start | bytes 24584 | tf_op jit(solution)/shard_map/ppermute | solution.py:12
  323.5 117.7 %collective-permute-start.7 = (f32[2048]{0:T(1024)S(1)}, f32[2048]{0:T(1024)S(1)}, u32[]{:S(2)}, u32[]{:S(2)}) collective-permute-start(f32[2048]{0:T(1024)S(1)} %add.46), channel_id=1, source_target_pairs={{2,0},{3,1},{4,2},{5,3},{6,4},{7,5},{8,6},{9,7},{10,8},{11,9},{12,... | collective-permute-start | bytes 24584 | tf_op jit(solution)/shard_map/ppermute | solution.py:12
where the time goes:
time: 445 us
  waiting for transfers between devices  381 us (86%)
  matrix products  23.7 us (5%)
  starting transfers between devices  17.4 us (4%)
  local copies, waits for them, and re-layouts  14.9 us (3%)
  other arithmetic  7.09 us (2%)
    ppermute x8, waiting for transfers between devices, from_behind(): return lax.ppermute(block, axis, route)  353 us
    all_to_all x1, waiting for transfers between devices, body(): lax.all_to_all(send_rows, 'blk', split_axis=0, concat_axis=0, tiled=True)  24.4 us
    dot_general x3, matrix products, contribute(): scores = jnp.dot(rows, panel.T, preferred_element_type=jnp.float32) * scale  13.2 us
    all_to_all x1, starting transfers between devices, body(): lax.all_to_all(send_lse, 'blk', split_axis=0, concat_axis=0, tiled=True)  11.1 us
    dot_general x3, matrix products, contribute(): lax.dot_general(resp_low, rows, (((0,), (0,)), ((), ())), preferred_eleme...  10.5 us
  transfers between devices with their start and end apart: 10, of which 7 were waited for; matrix products, arithmetic and copies ran while one was open for 4% of the time, Pallas kernels for 0%

commit v1 on v0

v1 whole, which is shorter than its diff:
```python
import functools

import jax
import jax.numpy as jnp
import ml_dtypes
import numpy as np
from jax import lax
from jax.experimental import pallas as pl
from jax.experimental.pallas import tpu as pltpu
from jax.sharding import PartitionSpec as P

MESH = pl.DeviceIdType.MESH
SIDE = 4
CAP = 5
EMPTY = 9984.0
GROUP = 16
CHUNKS = 6
BLOCK = 32
SLOTS = GROUP * CAP
TILE = 512


def hops(off):
    return sum(min(step, SIDE - step) for step in off)


OFFSETS = sorted(
    [(x, z, y) for x in range(SIDE) for z in range(SIDE) for y in range(SIDE) if x + z + y > 0],
    key=lambda off: -hops(off),
)


def packing():
    pack = np.zeros((GROUP * BLOCK, (CHUNKS + 1) * SLOTS), np.float32)
    for peer in range(GROUP):
        for slot in range(CAP):
            for chunk in range(CHUNKS):
                pack[peer * BLOCK + chunk * CAP + slot, chunk * SLOTS + peer * CAP + slot] = 1
            pack[peer * BLOCK + CHUNKS * CAP, CHUNKS * SLOTS + peer * CAP + slot] = 1
    lane = np.zeros((SLOTS, 128), np.float32)
    for row in range(SLOTS):
        lane[row, row % CAP] = 1
    return pack, lane


def kernel(
    rows_hbm, dest_hbm, lse_hbm, pack_hbm, unpack_hbm, lane_hbm, panel_hbm, out_hbm,
    rows, dest, lse, pack, unpack, lane, panel, out,
    stack, send, recv, swap, x_ref, l_ref, total, mass,
    in_sem, out_sem, send_sem, recv_sem, swap_send, swap_recv,
):
    me = lax.axis_index("blk")
    core = lax.rem(me, 2)
    chip = me // 2
    y = lax.rem(chip, SIDE)
    z = lax.rem(chip // SIDE, SIDE)
    x = chip // (SIDE * SIDE)
    other = me + 1 - 2 * core
    n = len(OFFSETS)
    devices = 2 * SIDE**3
    pool, width = rows.shape

    def chip_at(off):
        return (lax.rem(x + off[0], SIDE) * SIDE + lax.rem(z + off[1], SIDE)) * SIDE + lax.rem(y + off[2], SIDE)

    barrier = pltpu.get_barrier_semaphore()
    pl.semaphore_signal(barrier, inc=1, device_id=(other,), device_id_type=MESH)
    for off in OFFSETS:
        pl.semaphore_signal(barrier, inc=1, device_id=(2 * chip_at(off) + core,), device_id_type=MESH)

    loads = [
        pltpu.make_async_copy(src, dst, in_sem.at[i])
        for i, (src, dst) in enumerate(
            [(dest_hbm, dest), (rows_hbm, rows), (lse_hbm, lse), (pack_hbm, pack), (lane_hbm, lane), (unpack_hbm, unpack), (panel_hbm, panel)]
        )
    ]
    for load in loads:
        load.start()

    loads[0].wait()
    to = dest[...]
    hot = lax.broadcasted_iota(jnp.int32, (devices, pool), 0) == to
    earlier = lax.broadcasted_iota(jnp.int32, (pool, pool), 0) < lax.broadcasted_iota(jnp.int32, (pool, pool), 1)
    before = jnp.dot(hot.astype(jnp.bfloat16), earlier.astype(jnp.bfloat16), preferred_element_type=jnp.float32)
    rank = jnp.sum(jnp.where(hot, before, 0.0), axis=0, keepdims=True).astype(jnp.int32)
    slot = to * CAP + rank
    picks = lax.broadcasted_iota(jnp.int32, (devices * CAP, pool), 0) == slot
    loads[1].wait()
    sorted_rows = jnp.dot(picks.astype(jnp.bfloat16), rows[...], preferred_element_type=jnp.float32).astype(jnp.bfloat16)
    loads[2].wait()
    norm = lse[...].astype(jnp.float32) - EMPTY
    norms = jnp.sum(jnp.where(picks, norm, 0.0), axis=1, keepdims=True) + EMPTY
    loads[3].wait()
    loads[4].wait()
    for g in range(devices // GROUP):
        part = slice(g * SLOTS, (g + 1) * SLOTS)
        lanes = slice(g * 128, (g + 1) * 128)
        for j in range(CHUNKS):
            stack[j * SLOTS : (j + 1) * SLOTS, lanes] = sorted_rows[part, j * 128 : (j + 1) * 128]
        stack[CHUNKS * SLOTS :, lanes] = (norms[part] * lane[...].astype(jnp.float32)).astype(jnp.bfloat16)
    for h in range(devices // GROUP // 2):
        packed = jnp.dot(pack[...], stack[:, h * 256 : (h + 1) * 256], preferred_element_type=jnp.float32).astype(jnp.bfloat16)
        for i in range(2):
            g = 2 * h + i
            send[g * GROUP : (g + 1) * GROUP] = packed[:, i * 128 : (i + 1) * 128].reshape(GROUP, BLOCK, 128)
        if h == 0:
            send[devices : devices + 2] = packed[: 2 * BLOCK, :128].reshape(2, BLOCK, 128)

    pl.semaphore_wait(barrier, n + 1)
    for i, off in enumerate(OFFSETS):
        to_chip = chip_at(off)
        pltpu.make_async_remote_copy(
            src_ref=send.at[pl.ds(2 * to_chip, 4)],
            dst_ref=recv.at[i],
            send_sem=send_sem,
            recv_sem=recv_sem.at[i // GROUP],
            device_id=(2 * to_chip + core,),
            device_id_type=MESH,
        ).start()
    recv[n] = send[pl.ds(2 * chip, 4)]

    x_ref[...] = jnp.zeros_like(x_ref)
    empty = lax.broadcasted_iota(jnp.int32, (16, 128), 1) == 0
    l_ref[3 * SLOTS :] = jnp.where(empty, EMPTY, 0.0).astype(jnp.bfloat16)
    total[...] = jnp.zeros_like(total)
    mass[...] = jnp.zeros_like(mass)
    log2e = 1.4426950408889634
    scale = float(width) ** -0.5 * log2e
    loads[5].wait()
    loads[6].wait()

    def unpacked(block):
        packed = jnp.concatenate([block[:, d].reshape(GROUP * BLOCK, 128) for d in range(3)], axis=1)
        wide = jnp.dot(unpack[...], packed, preferred_element_type=jnp.float32).astype(jnp.bfloat16)
        for d in range(3):
            part = slice(d * SLOTS, (d + 1) * SLOTS)
            lanes = slice(d * 128, (d + 1) * 128)
            for j in range(CHUNKS):
                x_ref[part, j * 128 : (j + 1) * 128] = wide[j * SLOTS : (j + 1) * SLOTS, lanes]
            l_ref[part] = wide[CHUNKS * SLOTS :, lanes] * lane[...]
        norm = lax.dot_general(
            jnp.ones((8, 128), jnp.bfloat16), l_ref[...], (((1,), (1,)), ((), ())), preferred_element_type=jnp.float32
        )
        return norm[0:1] * log2e

    def contribute(block, last):
        norm = unpacked(block)
        xs = x_ref[...]
        for t in range(panel.shape[0] // TILE):
            tile = slice(t * TILE, (t + 1) * TILE)
            score = lax.dot_general(panel[tile], xs, (((1,), (1,)), ((), ())), preferred_element_type=jnp.float32)
            resp = jnp.exp2(score * scale - norm)
            count = resp[:, :128] + resp[:, 128:] + mass[tile]
            add = jnp.dot(resp.astype(jnp.bfloat16), xs, preferred_element_type=jnp.float32)
            if not last:
                mass[tile] = count
                total[tile] += add
            else:
                inverse = 1.0 / (jnp.sum(count, axis=1, keepdims=True) + 1.0)
                fresh = (total[tile] + add + panel[tile].astype(jnp.float32)) * inverse
                out[tile] = fresh.astype(jnp.bfloat16)
                pltpu.make_async_copy(out.at[tile], out_hbm.at[tile], out_sem.at[t]).start()

    groups = (n + 1) // GROUP
    for g in range(groups):
        arrived = recv.at[pl.ds(g * GROUP, GROUP if g < groups - 1 else GROUP - 1)]
        pltpu.make_async_copy(arrived, arrived, recv_sem.at[g]).wait()
        handed = pltpu.make_async_remote_copy(
            src_ref=recv.at[pl.ds(g * GROUP, GROUP), pl.ds(1 - core, 3)],
            dst_ref=swap.at[pl.ds(g * GROUP, GROUP)],
            send_sem=swap_send.at[g],
            recv_sem=swap_recv.at[g],
            device_id=(other,),
            device_id_type=MESH,
        )
        handed.start()
        contribute(recv[pl.ds(g * GROUP, GROUP), pl.ds(core, 3)], False)
        handed.wait()
        contribute(swap[pl.ds(g * GROUP, GROUP)], g == groups - 1)

    sent = recv.at[pl.ds(0, n)]
    pltpu.make_async_copy(sent, sent, send_sem).wait()
    for t in range(panel.shape[0] // TILE):
        tile = slice(t * TILE, (t + 1) * TILE)
        pltpu.make_async_copy(out.at[tile], out_hbm.at[tile], out_sem.at[t]).wait()


def body(embeddings, log_norms, destinations, centroids):
    devices = lax.axis_size("blk")
    pool, width = embeddings.shape
    panel = centroids.shape[0]
    pack, lane = packing()
    bf16 = jnp.bfloat16
    chips = len(OFFSETS) + 1
    groups = chips // GROUP
    any_spec = pl.BlockSpec(memory_space=pl.ANY)
    return pl.pallas_call(
        kernel,
        out_shape=jax.ShapeDtypeStruct((panel, width), bf16),
        in_specs=[any_spec] * 7,
        out_specs=any_spec,
        scratch_shapes=[
            pltpu.VMEM((pool, width), bf16),
            pltpu.VMEM((1, pool), jnp.int32),
            pltpu.VMEM((1, pool), jnp.float32),
            pltpu.VMEM(pack.shape, bf16),
            pltpu.VMEM(pack.shape[::-1], bf16),
            pltpu.VMEM(lane.shape, bf16),
            pltpu.VMEM((panel, width), bf16),
            pltpu.VMEM((panel, width), bf16),
            pltpu.VMEM(((CHUNKS + 1) * SLOTS, devices // GROUP * 128), bf16),
            pltpu.VMEM((devices + 2, BLOCK, 128), bf16),
            pltpu.VMEM((chips, 4, BLOCK, 128), bf16),
            pltpu.VMEM((chips, 3, BLOCK, 128), bf16),
            pltpu.VMEM((256, width), bf16),
            pltpu.VMEM((256, 128), bf16),
            pltpu.VMEM((panel, width), jnp.float32),
            pltpu.VMEM((panel, 128), jnp.float32),
            pltpu.SemaphoreType.DMA((7,)),
            pltpu.SemaphoreType.DMA((panel // TILE,)),
            pltpu.SemaphoreType.DMA,
            pltpu.SemaphoreType.DMA((groups,)),
            pltpu.SemaphoreType.DMA((groups,)),
            pltpu.SemaphoreType.DMA((groups,)),
        ],
        compiler_params=pltpu.CompilerParams(
            collective_id=0, has_side_effects=True, vmem_limit_bytes=48 * 2**20
        ),
        cost_estimate=pl.CostEstimate(
            flops=4 * 3 * CAP * devices * panel * width,
            bytes_accessed=4 * panel * width,
            transcendentals=3 * CAP * devices * panel,
        ),
    )(
        embeddings,
        destinations.reshape(1, pool),
        log_norms.astype(jnp.float32).reshape(1, pool),
        jnp.asarray(pack.astype(ml_dtypes.bfloat16)),
        jnp.asarray(pack.T.astype(ml_dtypes.bfloat16)),
        jnp.asarray(lane.astype(ml_dtypes.bfloat16)),
        centroids,
    )


def solution(mesh):
    return jax.shard_map(
        body,
        mesh=mesh,
        in_specs=(P("blk", None), P("blk"), P("blk", None), P("blk", None)),
        out_specs=P("blk", None),
        check_vma=False,
    )
```

time: 445 us -> 63.1 us (0.14)
  the two profiles are of different devices: /device:TPU:0 before, /device:TPU:2 now
where the time goes in v1:
time: 63.1 us; the launch traced here: 62.7 us
  Pallas kernels  55.8 us (88%)
  local copies, waits for them, and re-layouts  6.96 us (11%)
    pallas_call x1, Pallas kernels, body(): pl.pallas_call(kernel, out_shape=jax.ShapeDtypeStruct((panel, width), bf1...  55.8 us
    unnamed x11, local copies, waits for them, and re-layouts  6.28 us

profile of v1, /device:TPU:2, one launch (start us, length us, event | category | flops | bytes accessed | tf_op | source)
XLA Modules:
  0.0 62.7 jit_solution(628096550272466274)
XLA Ops:
  0.0 0.7 %reshape.12.lse_hbm = f32[1,384]{1,0:T(1,128)S(1)} reshape(bf16[384]{0:T(512)(128)(2,1)} %param.8) | data formatting | bytes 2304 | tf_op jit(solution)/shard_map/reshape | solution.py:237
  0.7 0.0 copy-start
  0.7 1.1 %copy-done = bf16[384,768]{1,0:T(8,128)(2,1)S(1)} copy-done((bf16[384,768]{1,0:T(8,128)(2,1)S(1)}, bf16[384,768]{1,0:T(8,128)(2,1)}, u32[]{:S(2)}) %copy-start) | copy-done | bytes 589848
  1.7 0.0 copy-start.1
  1.7 0.7 %copy-done.1 = s32[384,1]{0,1:T(1,128)S(1)} copy-done((s32[384,1]{0,1:T(1,128)S(1)}, s32[384,1]{0,1:T(1,128)}, u32[]{:S(2)}) %copy-start.1) | copy-done | bytes 1560
  2.4 0.0 copy-start.2
  2.4 1.1 %copy-done.2 = bf16[512,560]{1,0:T(8,128)(2,1)S(1)} copy-done((bf16[512,560]{1,0:T(8,128)(2,1)S(1)}, bf16[512,560]{1,0:T(8,128)(2,1)}, u32[]{:S(2)}) %copy-start.2) | copy-done | bytes 573464
  3.5 0.0 copy-start.3
  3.5 1.1 %copy-done.3 = bf16[560,512]{1,0:T(8,128)(2,1)S(1)} copy-done((bf16[560,512]{1,0:T(8,128)(2,1)S(1)}, bf16[560,512]{1,0:T(8,128)(2,1)}, u32[]{:S(2)}) %copy-start.3) | copy-done | bytes 573464
  4.6 0.0 copy-start.4
  4.6 0.7 %copy-done.4 = bf16[80,128]{1,0:T(8,128)(2,1)S(1)} copy-done((bf16[80,128]{1,0:T(8,128)(2,1)S(1)}, bf16[80,128]{1,0:T(8,128)(2,1)}, u32[]{:S(2)}) %copy-start.4) | copy-done | bytes 20504
  5.3 55.8 %shard_map.73 = bf16[2048,768]{1,0:T(8,128)(2,1)S(1)} custom-call(bf16[384,768]{1,0:T(8,128)(2,1)S(1)} %copy-done, s32[1,384]{1,0:T(1,128)S(1)} %bitcast.1, f32[1,384]{1,0:T(1,128)S(1)} %reshape.12.lse_hbm, bf16[512,560]{1,0:T(8,128)(2,1)S(1)} %copy-done.2, bf16[560,512]{1,0:T(8,128)(2,1)S(1)} %copy-done.3, bf16[80,128]{1,0:T(8,128)(2,1)S(1)} %copy-done.4, ...), custom_call_target="tpu_custom_call" | custom-call | flops 12079595520 | bytes 6291456 | tf_op jit(solution)/shard_map/pallas_call | solution.py:197
  61.1 1.7 %copy.9 = bf16[2048,768]{1,0:T(8,128)(2,1)} copy(bf16[2048,768]{1,0:T(8,128)(2,1)S(1)} %shard_map.73) | data formatting | bytes 6291456
Async XLA Ops:
  0.7 1.1 %copy-start = (bf16[384,768]{1,0:T(8,128)(2,1)S(1)}, bf16[384,768]{1,0:T(8,128)(2,1)}, u32[]{:S(2)}) copy-start(bf16[384,768]{1,0:T(8,128)(2,1)} %rows_hbm.1) | copy-start | bytes 1769476
  1.7 0.7 %copy-start.1 = (s32[384,1]{0,1:T(1,128)S(1)}, s32[384,1]{0,1:T(1,128)}, u32[]{:S(2)}) copy-start(s32[384,1]{0,1:T(1,128)} %param.9) | copy-start | bytes 4612
  2.4 1.1 %copy-start.2 = (bf16[512,560]{1,0:T(8,128)(2,1)S(1)}, bf16[512,560]{1,0:T(8,128)(2,1)}, u32[]{:S(2)}) copy-start(bf16[512,560]{1,0:T(8,128)(2,1)} %constant.6.clone.pack_hbm) | copy-start | bytes 1720324
  3.5 1.1 %copy-start.3 = (bf16[560,512]{1,0:T(8,128)(2,1)S(1)}, bf16[560,512]{1,0:T(8,128)(2,1)}, u32[]{:S(2)}) copy-start(bf16[560,512]{1,0:T(8,128)(2,1)} %constant.7.clone.unpack_hbm) | copy-start | bytes 1720324
  4.6 0.7 %copy-start.4 = (bf16[80,128]{1,0:T(8,128)(2,1)S(1)}, bf16[80,128]{1,0:T(8,128)(2,1)}, u32[]{:S(2)}) copy-start(bf16[80,128]{1,0:T(8,128)(2,1)} %constant.8.clone.lane_hbm) | copy-start | bytes 61444

commit v2 on v1

--- a/solution.py
+++ b/solution.py
@@ -1,9 +1,5 @@
-import functools
-
 import jax
 import jax.numpy as jnp
-import ml_dtypes
-import numpy as np
 from jax import lax
 from jax.experimental import pallas as pl
 from jax.experimental.pallas import tpu as pltpu
@@ -17,34 +13,35 @@
 CHUNKS = 6
 BLOCK = 32
 SLOTS = GROUP * CAP
-TILE = 512
+TILE = 256
+WINDOW = 2
 
 
 def hops(off):
     return sum(min(step, SIDE - step) for step in off)
 
 
+def ORDER(off):
+    return (-sum(off) % SIDE == 0, sum(off) % SIDE, -hops(off))
+
+
 OFFSETS = sorted(
     [(x, z, y) for x in range(SIDE) for z in range(SIDE) for y in range(SIDE) if x + z + y > 0],
-    key=lambda off: -hops(off),
+    key=ORDER,
 )
 
 
-def packing():
-    pack = np.zeros((GROUP * BLOCK, (CHUNKS + 1) * SLOTS), np.float32)
-    for peer in range(GROUP):
-        for slot in range(CAP):
-            for chunk in range(CHUNKS):
-                pack[peer * BLOCK + chunk * CAP + slot, chunk * SLOTS + peer * CAP + slot] = 1
-            pack[peer * BLOCK + CHUNKS * CAP, CHUNKS * SLOTS + peer * CAP + slot] = 1
-    lane = np.zeros((SLOTS, 128), np.float32)
-    for row in range(SLOTS):
-        lane[row, row % CAP] = 1
-    return pack, lane
+def packing(shape, stacked_dim):
+    stacked = lax.broadcasted_iota(jnp.int32, shape, stacked_dim)
+    chunk = sum([(stacked >= j * SLOTS).astype(jnp.int32) for j in range(1, CHUNKS + 1)])
+    inside = stacked - chunk * SLOTS
+    peer = (inside * 6554) >> 15
+    row = jnp.where(chunk < CHUNKS, chunk * CAP + inside - peer * CAP, CHUNKS * CAP)
+    return peer * BLOCK + row
 
 
 def kernel(
-    rows_hbm, dest_hbm, lse_hbm, pack_hbm, unpack_hbm, lane_hbm, panel_hbm, out_hbm,
+    rows_hbm, dest_hbm, lse_hbm, panel_hbm, out_hbm,
     rows, dest, lse, pack, unpack, lane, panel, out,
     stack, send, recv, swap, x_ref, l_ref, total, mass,
     in_sem, out_sem, send_sem, recv_sem, swap_send, swap_recv,
@@ -57,6 +54,7 @@
     x = chip // (SIDE * SIDE)
     other = me + 1 - 2 * core
     n = len(OFFSETS)
+    groups = (n + 1) // GROUP
     devices = 2 * SIDE**3
     pool, width = rows.shape
 
@@ -71,11 +69,21 @@
     loads = [
         pltpu.make_async_copy(src, dst, in_sem.at[i])
         for i, (src, dst) in enumerate(
-            [(dest_hbm, dest), (rows_hbm, rows), (lse_hbm, lse), (pack_hbm, pack), (lane_hbm, lane), (unpack_hbm, unpack), (panel_hbm, panel)]
+            [(dest_hbm, dest), (rows_hbm, rows), (lse_hbm, lse), (panel_hbm, panel)]
         )
     ]
     for load in loads:
         load.start()
+
+    depth = (CHUNKS + 1) * SLOTS
+    wide = GROUP * BLOCK
+    stacked = packing((8, depth), 1)[0:1]
+    pack[...] = (lax.broadcasted_iota(jnp.int32, (wide, depth), 0) == stacked).astype(jnp.bfloat16)
+    stacked = packing((depth, 128), 0)[:, 0:1]
+    unpack[...] = (lax.broadcasted_iota(jnp.int32, (depth, wide), 1) == stacked).astype(jnp.bfloat16)
+    row = lax.broadcasted_iota(jnp.int32, (SLOTS, 128), 0)
+    own_lane = lax.broadcasted_iota(jnp.int32, (SLOTS, 128), 1) == row - ((row * 6554) >> 15) * CAP
+    lane[...] = own_lane.astype(jnp.bfloat16)
 
     loads[0].wait()
     to = dest[...]
@@ -90,8 +98,6 @@
     loads[2].wait()
     norm = lse[...].astype(jnp.float32) - EMPTY
     norms = jnp.sum(jnp.where(picks, norm, 0.0), axis=1, keepdims=True) + EMPTY
-    loads[3].wait()
-    loads[4].wait()
     for g in range(devices // GROUP):
         part = slice(g * SLOTS, (g + 1) * SLOTS)
         lanes = slice(g * 128, (g + 1) * 128)
@@ -107,16 +113,20 @@
             send[devices : devices + 2] = packed[: 2 * BLOCK, :128].reshape(2, BLOCK, 128)
 
     pl.semaphore_wait(barrier, n + 1)
-    for i, off in enumerate(OFFSETS):
-        to_chip = chip_at(off)
-        pltpu.make_async_remote_copy(
-            src_ref=send.at[pl.ds(2 * to_chip, 4)],
-            dst_ref=recv.at[i],
-            send_sem=send_sem,
-            recv_sem=recv_sem.at[i // GROUP],
-            device_id=(2 * to_chip + core,),
-            device_id_type=MESH,
-        ).start()
+    def dispatch(g):
+        for i in range(g * GROUP, min((g + 1) * GROUP, n)):
+            to_chip = chip_at(OFFSETS[i])
+            pltpu.make_async_remote_copy(
+                src_ref=send.at[pl.ds(2 * to_chip, 4)],
+                dst_ref=recv.at[i],
+                send_sem=send_sem,
+                recv_sem=recv_sem.at[g],
+                device_id=(2 * to_chip + core,),
+                device_id_type=MESH,
+            ).start()
+
+    for g in range(WINDOW):
+        dispatch(g)
     recv[n] = send[pl.ds(2 * chip, 4)]
 
     x_ref[...] = jnp.zeros_like(x_ref)
@@ -126,8 +136,7 @@
     mass[...] = jnp.zeros_like(mass)
     log2e = 1.4426950408889634
     scale = float(width) ** -0.5 * log2e
-    loads[5].wait()
-    loads[6].wait()
+    loads[3].wait()
 
     def unpacked(block):
         packed = jnp.concatenate([block[:, d].reshape(GROUP * BLOCK, 128) for d in range(3)], axis=1)
@@ -161,10 +170,11 @@
                 out[tile] = fresh.astype(jnp.bfloat16)
                 pltpu.make_async_copy(out.at[tile], out_hbm.at[tile], out_sem.at[t]).start()
 
-    groups = (n + 1) // GROUP
     for g in range(groups):
         arrived = recv.at[pl.ds(g * GROUP, GROUP if g < groups - 1 else GROUP - 1)]
         pltpu.make_async_copy(arrived, arrived, recv_sem.at[g]).wait()
+        if g + WINDOW < groups:
+            dispatch(g + WINDOW)
         handed = pltpu.make_async_remote_copy(
             src_ref=recv.at[pl.ds(g * GROUP, GROUP), pl.ds(1 - core, 3)],
             dst_ref=swap.at[pl.ds(g * GROUP, GROUP)],
@@ -189,7 +199,7 @@
     devices = lax.axis_size("blk")
     pool, width = embeddings.shape
     panel = centroids.shape[0]
-    pack, lane = packing()
+    depth, wide = (CHUNKS + 1) * SLOTS, GROUP * BLOCK
     bf16 = jnp.bfloat16
     chips = len(OFFSETS) + 1
     groups = chips // GROUP
@@ -197,18 +207,18 @@
     return pl.pallas_call(
         kernel,
         out_shape=jax.ShapeDtypeStruct((panel, width), bf16),
-        in_specs=[any_spec] * 7,
+        in_specs=[any_spec] * 4,
         out_specs=any_spec,
         scratch_shapes=[
             pltpu.VMEM((pool, width), bf16),
             pltpu.VMEM((1, pool), jnp.int32),
             pltpu.VMEM((1, pool), jnp.float32),
-            pltpu.VMEM(pack.shape, bf16),
-            pltpu.VMEM(pack.shape[::-1], bf16),
-            pltpu.VMEM(lane.shape, bf16),
+            pltpu.VMEM((wide, depth), bf16),
+            pltpu.VMEM((depth, wide), bf16),
+            pltpu.VMEM((SLOTS, 128), bf16),
             pltpu.VMEM((panel, width), bf16),
             pltpu.VMEM((panel, width), bf16),
-            pltpu.VMEM(((CHUNKS + 1) * SLOTS, devices // GROUP * 128), bf16),
+            pltpu.VMEM((depth, devices // GROUP * 128), bf16),
             pltpu.VMEM((devices + 2, BLOCK, 128), bf16),
             pltpu.VMEM((chips, 4, BLOCK, 128), bf16),
             pltpu.VMEM((chips, 3, BLOCK, 128), bf16),
@@ -216,7 +226,7 @@
             pltpu.VMEM((256, 128), bf16),
             pltpu.VMEM((panel, width), jnp.float32),
             pltpu.VMEM((panel, 128), jnp.float32),
-            pltpu.SemaphoreType.DMA((7,)),
+            pltpu.SemaphoreType.DMA((4,)),
             pltpu.SemaphoreType.DMA((panel // TILE,)),
             pltpu.SemaphoreType.DMA,
             pltpu.SemaphoreType.DMA((groups,)),
@@ -224,7 +234,7 @@
             pltpu.SemaphoreType.DMA((groups,)),
         ],
         compiler_params=pltpu.CompilerParams(
-            collective_id=0, has_side_effects=True, vmem_limit_bytes=48 * 2**20
+            collective_id=0, has_side_effects=True, vmem_limit_bytes=63 * 2**20
         ),
         cost_estimate=pl.CostEstimate(
             flops=4 * 3 * CAP * devices * panel * width,
@@ -235,9 +245,6 @@
         embeddings,
         destinations.reshape(1, pool),
         log_norms.astype(jnp.float32).reshape(1, pool),
-        jnp.asarray(pack.astype(ml_dtypes.bfloat16)),
-        jnp.asarray(pack.T.astype(ml_dtypes.bfloat16)),
-        jnp.asarray(lane.astype(ml_dtypes.bfloat16)),
         centroids,
     )
 

time: 63.1 us -> 51.9 us (0.82)
  the two profiles are of different devices: /device:TPU:2 before, /device:TPU:0 now
where the time goes in v2:
time: 51.9 us; the launch traced here: 51.8 us
  Pallas kernels  46.8 us (90%)
  local copies, waits for them, and re-layouts  5 us (10%)
    pallas_call x1, Pallas kernels, body(): pl.pallas_call(kernel, out_shape=jax.ShapeDtypeStruct((panel, width), bf1...  46.8 us
    unnamed x1, local copies, waits for them, and re-layouts  3.76 us
    reshape x1, local copies, waits for them, and re-layouts, body(): log_norms.astype(jnp.float32).reshape(1, pool)  1.24 us

profile of v2, /device:TPU:0, one launch (start us, length us, event | category | flops | bytes accessed | tf_op | source)
XLA Modules:
  0.0 51.8 jit_solution(14567615426717022753)
XLA Ops:
  0.0 1.2 %reshape.12.lse_hbm = f32[1,384]{1,0:T(1,128)} reshape(bf16[384]{0:T(512)(128)(2,1)} %param.5) | data formatting | bytes 2304 | tf_op jit(solution)/shard_map/reshape | solution.py:247
  1.2 46.8 %shard_map.46 = bf16[2048,768]{1,0:T(8,128)(2,1)} custom-call(bf16[384,768]{1,0:T(8,128)(2,1)} %rows_hbm.1, s32[1,384]{1,0:T(1,128)} %bitcast.1, f32[1,384]{1,0:T(1,128)} %reshape.12.lse_hbm, bf16[2048,768]{1,0:T(8,128)(2,1)} %panel_hbm.1), custom_call_target="tpu_custom_call" | custom-call | flops 12079595520 | bytes 6291456 | tf_op jit(solution)/shard_map/pallas_call | solution.py:207
  48.0 3.8 %copy.6 = bf16[2048,768]{1,0:T(8,128)(2,1)} copy(bf16[2048,768]{1,0:T(8,128)(2,1)} %shard_map.46) | data formatting | bytes 6291456

commit v3 on v2

--- a/solution.py
+++ b/solution.py
@@ -41,10 +41,10 @@
 
 
 def kernel(
-    rows_hbm, dest_hbm, lse_hbm, panel_hbm, out_hbm,
-    rows, dest, lse, pack, unpack, lane, panel, out,
+    rows_hbm, dest_hbm, lse_hbm, panel_hbm, out,
+    rows, dest, lse, pack, unpack, lane, panel,
     stack, send, recv, swap, x_ref, l_ref, total, mass,
-    in_sem, out_sem, send_sem, recv_sem, swap_send, swap_recv,
+    in_sem, send_sem, recv_sem, swap_send, swap_recv,
 ):
     me = lax.axis_index("blk")
     core = lax.rem(me, 2)
@@ -59,7 +59,8 @@
     pool, width = rows.shape
 
     def chip_at(off):
-        return (lax.rem(x + off[0], SIDE) * SIDE + lax.rem(z + off[1], SIDE)) * SIDE + lax.rem(y + off[2], SIDE)
+        a, b, c = (first + core * (second - first) for first, second in zip(off, off[1:] + off[:1]))
+        return (lax.rem(x + a, SIDE) * SIDE + lax.rem(z + b, SIDE)) * SIDE + lax.rem(y + c, SIDE)
 
     barrier = pltpu.get_barrier_semaphore()
     pl.semaphore_signal(barrier, inc=1, device_id=(other,), device_id_type=MESH)
@@ -96,7 +97,7 @@
     loads[1].wait()
     sorted_rows = jnp.dot(picks.astype(jnp.bfloat16), rows[...], preferred_element_type=jnp.float32).astype(jnp.bfloat16)
     loads[2].wait()
-    norm = lse[...].astype(jnp.float32) - EMPTY
+    norm = lse[...].reshape(1, pool).astype(jnp.float32) - EMPTY
     norms = jnp.sum(jnp.where(picks, norm, 0.0), axis=1, keepdims=True) + EMPTY
     for g in range(devices // GROUP):
         part = slice(g * SLOTS, (g + 1) * SLOTS)
@@ -168,7 +169,6 @@
                 inverse = 1.0 / (jnp.sum(count, axis=1, keepdims=True) + 1.0)
                 fresh = (total[tile] + add + panel[tile].astype(jnp.float32)) * inverse
                 out[tile] = fresh.astype(jnp.bfloat16)
-                pltpu.make_async_copy(out.at[tile], out_hbm.at[tile], out_sem.at[t]).start()
 
     for g in range(groups):
         arrived = recv.at[pl.ds(g * GROUP, GROUP if g < groups - 1 else GROUP - 1)]
@@ -190,9 +190,6 @@
 
     sent = recv.at[pl.ds(0, n)]
     pltpu.make_async_copy(sent, sent, send_sem).wait()
-    for t in range(panel.shape[0] // TILE):
-        tile = slice(t * TILE, (t + 1) * TILE)
-        pltpu.make_async_copy(out.at[tile], out_hbm.at[tile], out_sem.at[t]).wait()
 
 
 def body(embeddings, log_norms, destinations, centroids):
@@ -203,20 +200,18 @@
     bf16 = jnp.bfloat16
     chips = len(OFFSETS) + 1
     groups = chips // GROUP
-    any_spec = pl.BlockSpec(memory_space=pl.ANY)
     return pl.pallas_call(
         kernel,
         out_shape=jax.ShapeDtypeStruct((panel, width), bf16),
-        in_specs=[any_spec] * 4,
-        out_specs=any_spec,
+        in_specs=[pl.BlockSpec(memory_space=pl.ANY)] * 4,
+        out_specs=pl.BlockSpec(memory_space=pltpu.VMEM),
         scratch_shapes=[
             pltpu.VMEM((pool, width), bf16),
             pltpu.VMEM((1, pool), jnp.int32),
-            pltpu.VMEM((1, pool), jnp.float32),
+            pltpu.VMEM((pool,), bf16),
             pltpu.VMEM((wide, depth), bf16),
             pltpu.VMEM((depth, wide), bf16),
             pltpu.VMEM((SLOTS, 128), bf16),
-            pltpu.VMEM((panel, width), bf16),
             pltpu.VMEM((panel, width), bf16),
             pltpu.VMEM((depth, devices // GROUP * 128), bf16),
             pltpu.VMEM((devices + 2, BLOCK, 128), bf16),
@@ -227,14 +222,13 @@
             pltpu.VMEM((panel, width), jnp.float32),
             pltpu.VMEM((panel, 128), jnp.float32),
             pltpu.SemaphoreType.DMA((4,)),
-            pltpu.SemaphoreType.DMA((panel // TILE,)),
             pltpu.SemaphoreType.DMA,
             pltpu.SemaphoreType.DMA((groups,)),
             pltpu.SemaphoreType.DMA((groups,)),
             pltpu.SemaphoreType.DMA((groups,)),
         ],
         compiler_params=pltpu.CompilerParams(
-            collective_id=0, has_side_effects=True, vmem_limit_bytes=63 * 2**20
+            collective_id=0, has_side_effects=True, vmem_limit_bytes=40 * 2**20
         ),
         cost_estimate=pl.CostEstimate(
             flops=4 * 3 * CAP * devices * panel * width,
@@ -242,10 +236,10 @@
             transcendentals=3 * CAP * devices * panel,
         ),
     )(
-        embeddings,
-        destinations.reshape(1, pool),
-        log_norms.astype(jnp.float32).reshape(1, pool),
-        centroids,
+        *[
+            pltpu.with_memory_space_constraint(operand, pltpu.HBM)
+            for operand in (embeddings, destinations.reshape(1, pool), log_norms, centroids)
+        ]
     )
 
 

time: 51.9 us -> 44.4 us (0.86)
  Pallas kernels: 46.8 us -> 42.6 us
  local copies, waits for them, and re-layouts: 5 us -> 1.67 us
    pallas_call x1, Pallas kernels: 46.8 us -> 42.6 us  [body(): pl.pallas_call(kernel, out_shape=jax.ShapeDtypeStruct((panel, width), bf1...]
    unnamed x1, local copies, waits for them, and re-layouts: 3.76 us -> 1.67 us
    reshape x1 -> x0, local copies, waits for them, and re-layouts: 1.24 us -> none  [body(): log_norms.astype(jnp.float32).reshape(1, pool)]
where the time goes in v3:
time: 44.4 us; the launch traced here: 44.3 us
  Pallas kernels  42.6 us (96%)
  local copies, waits for them, and re-layouts  1.67 us (4%)
    pallas_call x1, Pallas kernels, body(): pl.pallas_call(kernel, out_shape=jax.ShapeDtypeStruct((panel, width), bf1...  42.6 us
    unnamed x1, local copies, waits for them, and re-layouts  1.67 us

profile of v3, /device:TPU:0, one launch (start us, length us, event | category | flops | bytes accessed | tf_op | source)
XLA Modules:
  0.0 44.3 jit_solution(18249677920122434115)
XLA Ops:
  0.0 42.6 %shard_map.46 = bf16[2048,768]{1,0:T(8,128)(2,1)S(1)} custom-call(bf16[384,768]{1,0:T(8,128)(2,1)} %rows_hbm.1, s32[1,384]{1,0:T(1,128)} %bitcast.1, bf16[384]{0:T(512)(128)(2,1)} %lse_hbm.1, bf16[2048,768]{1,0:T(8,128)(2,1)} %panel_hbm.1), custom_call_target="tpu_custom_call" | custom-call | flops 12079595520 | bytes 6291456 | tf_op jit(solution)/shard_map/pallas_call | solution.py:203
  42.6 1.7 %copy.6 = bf16[2048,768]{1,0:T(8,128)(2,1)} copy(bf16[2048,768]{1,0:T(8,128)(2,1)S(1)} %shard_map.46) | data formatting | bytes 6291456

commit v4 on v3

--- a/solution.py
+++ b/solution.py
@@ -156,9 +156,17 @@
     def contribute(block, last):
         norm = unpacked(block)
         xs = x_ref[...]
+
+        def scores(t):
+            if t == panel.shape[0] // TILE:
+                return None
+            rows_of = panel[t * TILE : (t + 1) * TILE]
+            return lax.dot_general(rows_of, xs, (((1,), (1,)), ((), ())), preferred_element_type=jnp.float32)
+
+        ahead = scores(0)
         for t in range(panel.shape[0] // TILE):
             tile = slice(t * TILE, (t + 1) * TILE)
-            score = lax.dot_general(panel[tile], xs, (((1,), (1,)), ((), ())), preferred_element_type=jnp.float32)
+            score, ahead = ahead, scores(t + 1)
             resp = jnp.exp2(score * scale - norm)
             count = resp[:, :128] + resp[:, 128:] + mass[tile]
             add = jnp.dot(resp.astype(jnp.bfloat16), xs, preferred_element_type=jnp.float32)

time: 44.4 us -> 44.4 us (level)
  the two profiles are of different devices: /device:TPU:0 before, /device:TPU:48 now
where the time goes in v4:
time: 44.4 us; the launch traced here: 44.3 us
  Pallas kernels  42.6 us (96%)
  local copies, waits for them, and re-layouts  1.67 us (4%)
    pallas_call x1, Pallas kernels, body(): pl.pallas_call(kernel, out_shape=jax.ShapeDtypeStruct((panel, width), bf1...  42.6 us
    unnamed x1, local copies, waits for them, and re-layouts  1.67 us

profile of v4, /device:TPU:48, one launch (start us, length us, event | category | flops | bytes accessed | tf_op | source)
XLA Modules:
  0.0 44.3 jit_solution(11468085737532070994)
XLA Ops:
  0.0 42.6 %shard_map.46 = bf16[2048,768]{1,0:T(8,128)(2,1)S(1)} custom-call(bf16[384,768]{1,0:T(8,128)(2,1)} %rows_hbm.1, s32[1,384]{1,0:T(1,128)} %bitcast.1, bf16[384]{0:T(512)(128)(2,1)} %lse_hbm.1, bf16[2048,768]{1,0:T(8,128)(2,1)} %panel_hbm.1), custom_call_target="tpu_custom_call" | custom-call | flops 12079595520 | bytes 6291456 | tf_op jit(solution)/shard_map/pallas_call | solution.py:211
  42.6 1.7 %copy.6 = bf16[2048,768]{1,0:T(8,128)(2,1)} copy(bf16[2048,768]{1,0:T(8,128)(2,1)S(1)} %shard_map.46) | data formatting | bytes 6291456
